TPU v7x, 512 devices: a whole 4x4x16 slice. The times are simulated.
512 devices in a mesh: ctx: 32 (over z, core), inner: 16 (over y, x).
Axes of the slice: x: 4, y: 4, z: 16, core: 2. Of those that a mesh axis runs over, the one named last changes fastest.
Arguments:
- tokens: bfloat16 [65536, 2048], P(('ctx', 'inner')), may hold values from -6 to 6
- project_weight: bfloat16 [2048, 2, 4096], P('ctx', None, 'inner'), may hold values from -0.125 to 0.125
- state_weight: bfloat16 [2048, 2, 512], P('ctx', None, 'inner'), may hold values from -0.125 to 0.125
- step_weight: bfloat16 [2048, 64], P('ctx', 'inner'), may hold values from -0.125 to 0.125
- mixer_taps: float32 [5, 4096], P(None, 'inner'), may hold values from -2.5 to 2.5
- state_taps: float32 [5, 2, 512], replicated, may hold values from -2.5 to 2.5
- step_bias: float32 [64], P('inner'), may hold values from -4.6 to -2.3
- decay_log: float32 [64], P('inner'), may hold values from -13 to 0.5, as said below
- norm_gain: float32 [4096], replicated, may hold values from 0.1 to 1.9
Outputs:
- mixed_output: bfloat16 [65536, 4096], P(('ctx', 'inner'))
Inputs may be any that keep to these rules, and one draw needn't show every extreme that they name: `decay_log`: one value a head.
All inputs are finite; a program needn't handle non-finite values.
Results may differ from a plain program's by a relative error of at most 0.0075.
Values may be sent and summed in bfloat16 or wider, within the bound.
A program may use at most 64 MiB of HBM per device.

v0:
```python
import jax
import jax.numpy as jnp
from jax import lax
from jax.sharding import PartitionSpec as P

H = 64
P_SIZE = 64
N = 128
G = 4
CONV = 4
SPAN = 128
EPSILON = 1e-05


def passed_along(x, axis, by):
    count = lax.axis_size(axis)
    pairs = [(i, i + by) for i in range(count) if 0 <= i + by < count]
    return lax.ppermute(x, axis, pairs)


def entering(x, axis, join, neutral):
    place = lax.axis_index(axis)
    gathered = jax.tree.map(
        lambda a, kind: lax.all_gather(a.astype(kind), axis), x, (jnp.bfloat16, jnp.bfloat16)
    )
    state = jax.tree.map(lambda a, e: jnp.zeros_like(a) + jnp.asarray(e, a.dtype), x, neutral)

    def one(turn, state):
        return join(
            state,
            jax.tree.map(
                lambda a, own: lax.dynamic_index_in_dim(a, turn, 0, False).astype(own.dtype),
                gathered,
                x,
            ),
        )

    return lax.fori_loop(0, place, one, state)


def partner(value, axis, stride):
    mask = 2**stride
    pairs = [(source, source ^ mask) for source in range(lax.axis_size(axis))]
    return lax.ppermute(value, axis, pairs)


def conv_apply(taps, previous, current):
    extended = jnp.concatenate([previous, current], axis=0)
    length_rows = current.shape[0]
    mixed = jnp.broadcast_to(taps[CONV], current.shape)
    for offset in range(CONV):
        mixed = mixed + taps[offset] * extended[offset : offset + length_rows].astype(jnp.float32)
    return jax.nn.silu(mixed).astype(jnp.bfloat16)


def join_chain(earlier, later):
    return (earlier[0] + later[0], jnp.exp(later[0])[:, None, None] * earlier[1] + later[1])


def carry_block(state, inputs):
    decay_sum, added = inputs
    return (jnp.exp(decay_sum)[:, None, None] * state + added, state)


def pick_group(values, group):
    shaped = values.reshape(values.shape[:-1] + (N, G))
    return lax.dynamic_index_in_dim(shaped, group, shaped.ndim - 1, keepdims=False)


def on_device(
    tokens,
    project_weight,
    state_weight,
    step_weight,
    mixer_taps,
    state_taps,
    step_bias,
    decay_log,
    norm_gain,
):
    inner_id = lax.axis_index("inner")
    project_rows, state_rows, step_rows = (
        lax.all_gather(project_weight, "ctx", axis=0, tiled=True),
        lax.all_gather(state_weight, "ctx", axis=0, tiled=True),
        lax.all_gather(step_weight, "ctx", axis=0, tiled=True),
    )
    heads_here = step_weight.shape[1]
    width_here = project_weight.shape[2]
    model_width = project_rows.shape[0]
    group = inner_id * heads_here // (H // G)
    full_cols = lax.all_gather(state_rows, "inner", axis=2, tiled=True)
    slice_cols = N
    state_cols = pick_group(full_cols, group)
    state_conv = pick_group(state_taps, group)
    joined = jnp.concatenate(
        [
            project_rows.reshape(model_width, 2 * width_here),
            state_cols.reshape(model_width, 2 * slice_cols),
            step_rows,
        ],
        axis=1,
    )
    projected = jnp.dot(
        lax.all_gather(tokens, "inner", axis=0, tiled=True),
        joined,
        preferred_element_type=jnp.float32,
    ).astype(jnp.bfloat16)
    rows_total = projected.shape[0]
    gate_values = projected[:, :width_here]
    x_pre = projected[:, width_here : 2 * width_here]
    state_pre = projected[:, 2 * width_here : 2 * width_here + 2 * slice_cols].reshape(
        rows_total, 2, slice_cols
    )
    step_raw = projected[:, 2 * width_here + 2 * slice_cols :]
    edge_row = rows_total - (CONV - 1)
    prior_x, prior_state = passed_along((x_pre[edge_row:], state_pre[edge_row:]), "ctx", 1)
    x_vals = conv_apply(mixer_taps, prior_x, x_pre)
    state_vals = conv_apply(state_conv, prior_state, state_pre)
    blocks = rows_total // SPAN
    b_blocks = state_vals[:, 0].reshape(blocks, SPAN, N)
    c_blocks = state_vals[:, 1].reshape(blocks, SPAN, N)
    step_size = jax.nn.softplus(step_raw.astype(jnp.float32) + step_bias)
    step_heads = step_size.T.reshape(heads_here, blocks, SPAN)
    cumul = jnp.cumsum(step_heads * (-jnp.exp(decay_log))[:, None, None], axis=2)
    scores = jnp.einsum("ctn,csn->cts", c_blocks, b_blocks, preferred_element_type=jnp.float32)
    lower = jnp.tril(jnp.ones((SPAN, SPAN), dtype=bool))
    spacing = jnp.where(lower, cumul[..., :, None] - cumul[..., None, :], -jnp.inf)
    mixing = (scores[None] * jnp.exp(spacing) * step_heads[:, :, None, :]).astype(jnp.bfloat16)
    x_blocks = x_vals.reshape(blocks, SPAN, heads_here, P_SIZE)
    diagonal = jnp.einsum("hcts,cshp->cthp", mixing, x_blocks, preferred_element_type=jnp.float32)
    ending = cumul[:, :, -1]
    to_end = jnp.exp(ending[..., None] - cumul) * step_heads
    weighted_b = (b_blocks.astype(jnp.float32)[None] * to_end[..., None]).astype(jnp.bfloat16)
    fresh = jnp.einsum("hcsn,cshp->chnp", weighted_b, x_blocks, preferred_element_type=jnp.float32)
    empty_state = jnp.zeros((heads_here, N, P_SIZE), jnp.float32)
    block_state, local_in = lax.scan(carry_block, empty_state, (ending.T, fresh))
    block_log = jnp.sum(ending, axis=1)
    before_log = (jnp.cumsum(ending, axis=1) - ending).T
    _, prior_block = entering(
        (block_log, block_state), "ctx", join_chain, (jnp.zeros_like(block_log), empty_state)
    )
    state_in = local_in + jnp.exp(before_log)[:, :, None, None] * prior_block[None]
    c_scaled = (c_blocks.astype(jnp.float32)[None] * jnp.exp(cumul)[..., None]).astype(jnp.bfloat16)
    state_high = state_in.astype(jnp.bfloat16)
    state_low = (state_in - state_high.astype(jnp.float32)).astype(jnp.bfloat16)
    offdiag = jnp.einsum(
        "hctn,chnp->cthp", c_scaled, state_high, preferred_element_type=jnp.float32
    )
    offdiag = offdiag + jnp.einsum(
        "hctn,chnp->cthp", c_scaled, state_low, preferred_element_type=jnp.float32
    )
    outputs = (diagonal + offdiag).reshape(rows_total, width_here)
    gated = (outputs * jax.nn.silu(gate_values.astype(jnp.float32))).astype(jnp.bfloat16)
    gated_wide = gated.astype(jnp.float32)
    squares = jnp.sum(gated_wide * gated_wide, axis=1)
    group_devices = H // G // heads_here
    for bit in range(group_devices.bit_length() - 1):
        squares = squares + partner(squares, "inner", bit)
    power = squares[:, None] / (H * P_SIZE // G)
    gain_here = lax.dynamic_slice_in_dim(norm_gain, inner_id * width_here, width_here, 0)
    normed = (gated_wide * lax.rsqrt(power + EPSILON) * gain_here).astype(jnp.bfloat16)
    result = lax.all_to_all(normed, "inner", split_axis=0, concat_axis=1, tiled=True)
    return result


def solution(mesh):
    placed = (
        P(("ctx", "inner"), None),
        P("ctx", None, "inner"),
        P("ctx", None, "inner"),
        P("ctx", "inner"),
        P(None, "inner"),
        P(),
        P("inner"),
        P("inner"),
        P(),
    )
    return jax.shard_map(
        on_device, mesh=mesh, in_specs=placed, out_specs=P(("ctx", "inner"), None), check_vma=False
    )
```

profile of v0, /device:TPU:480, one launch (start us, length us, event | category | flops | bytes accessed | tf_op | source)
XLA Modules:
  0.0 455.8 jit_solution(17512234280697024061)
XLA Ops:
  8.1 30.7 %all_gather.26 = bf16[2048,2,32]{2,1,0:T(2,128)(2,1)S(1)} all-gather(bf16[64,2,32]{2,1,0:T(2,128)(2,1)S(1)} %copy.91), channel_id=1, replica_groups=mesh['ctx'=32,'inner'=16] {'ctx'}, dimensions={0}, use_global_device_ids=true | all-gather | bytes 270336 | tf_op jit(solution)/shard_map/all_gather | solution.py:84
  41.4 29.1 %all-gather.2 = bf16[32,64,4]{1,2,0:T(4,128)(2,1)S(1)} all-gather(bf16[1,64,4]{1,2,0:T(4,128)(2,1)S(1)} %bitcast.102), channel_id=1, replica_groups=mesh['ctx'=32,'inner'=16] {'ctx'}, dimensions={0}, use_global_device_ids=true | all-gather | bytes 16896 | tf_op jit(solution)/shard_map/all_gather | solution.py:85
  72.8 6.1 %all-gather.8.cloned.1.call-done = bf16[2048,2,256]{2,1,0:T(2,128)(2,1)} async-done(((bf16[64,2,256]{2,1,0:T(2,128)(2,1)}), bf16[2048,2,256]{2,1,0:T(2,128)(2,1)}) %all-gather.8.cloned.1.call-update) | async-done | bytes 2097168 | tf_op jit(solution)/shard_map/all_gather | solution.py:83
  78.9 2.0 copy.123
  81.0 66.3 %all-gather.10.cloned.1.call-done = bf16[2048,2,512]{0,1,2:T(2,128)(2,1)} async-done(((bf16[2048,2,32]{0,1,2:T(2,128)(2,1)}), bf16[2048,2,512]{0,1,2:T(2,128)(2,1)}) %all-gather.10.cloned.1.call-update) | async-done | bytes 4194320 | tf_op jit(solution)/shard_map/all_gather | solution.py:91
  147.3 1.9 constant_dynamic-slice_fusion.2
  150.9 85.3 %all-gather.12.cloned.1.call-done = bf16[2048,2048]{1,0:T(8,128)(2,1)} async-done(((bf16[128,2048]{1,0:T(8,128)(2,1)}), bf16[2048,2048]{1,0:T(8,128)(2,1)}) %all-gather.12.cloned.1.call-update) | async-done | bytes 8388624 | tf_op jit(solution)/shard_map/all_gather | solution.py:104
  236.1 10.8 %fusion.12 = bf16[2048,772]{0,1:T(8,128)(2,1)S(1)} fusion(bf16[2048,2048]{1,0:T(8,128)(2,1)} %all-gather.12.cloned.1.call-done, bf16[2048,4]{1,0:T(8,128)(2,1)} %bitcast.92, bf16[2048,256]{1,0:T(8,128)(2,1)} %copy.95, bf16[2048,512]{1,0:T(8,128)(2,1)S(1)} %bitcast.91), kind=kOutput, calls=%fused_computation.21 | convolution fusion | flops 6487072768 | bytes 14712832 | tf_op jit(solution)/shard_map/dot_general | solution.py:103
  252.2 2.1 collective-permute-start.1
  255.7 2.2 fusion.51
  258.2 2.2 multiply_convert_fusion.7
  260.8 3.9 fusion.26
  264.7 28.8 %while.26 = (s32[]{:T(128)}, f32[4,128,64]{2,1,0:T(8,128)S(1)}, f32[16,4,128,64]{3,2,1,0:T(8,128)}, f32[16,4]{1,0:T(8,128)S(1)}, f32[16,4,128,64]{3,2,1,0:T(8,128)}, /*index=5*/s32[]{:T(128)}, s32[]{:T(128)}) while((s32[]{:T(128)}, f32[4,128,64]{2,1,0:T(8,128)S(1)}, f32[16,4,128,64]{3,2,1,0:T(8,128)}, f32[16,4]{1,0:T(8,128)S(1)}, ...), condition=%wide.region_2.3_spmd.clone, body=%wide.region_1.2_spmd.clone.sunk | while | flops 131075 | bytes 787088 | solution.py:136
  296.8 42.4 %all-reduce = bf16[128]{0:T(256)(128)(2,1)S(1)} all-reduce(bf16[128]{0:T(256)(128)(2,1)S(1)} %dynamic-update-slice), channel_id=2, replica_groups=mesh['ctx'=32,'inner'=16] {'ctx'}, use_global_device_ids=true, to_apply=%add | all-reduce | flops 128 | bytes 512
  340.3 3.3 fusion.18
  343.6 22.2 %all-gather.14.cloned.1.call-done = bf16[128,128,64]{1,2,0:T(8,128)(2,1)} async-done(((bf16[4,128,64]{1,2,0:T(8,128)(2,1)}), bf16[128,128,64]{1,2,0:T(8,128)(2,1)}) %all-gather.14.cloned.1.call-update) | async-done | bytes 2097168 | tf_op jit(solution)/shard_map/all_gather | solution.py:24
  365.8 34.4 %while.25 = (s32[]{:T(128)}, f32[4,128,64]{2,1,0:T(8,128)S(1)}, s32[]{:T(128)}, bf16[32,4]{1,0:T(8,128)(2,1)S(1)}, bf16[32,4,128,64]{2,3,1,0:T(8,128)(2,1)}, /*index=5*/s32[]{:T(128)}, s32[]{:T(128)}, s32[]{:T(128)}) while((s32[]{:T(128)}, f32[4,128,64]{2,1,0:T(8,128)S(1)}, s32[]{:T(128)}, bf16[32,4]{1,0:T(8,128)(2,1)S(1)}, ...), condition=%wide.region_6.7_spmd, body=%wide.region_5.6_spmd.sunk | while | flops 98313 | bytes 589991 | solution.py:38
  400.2 5.2 %fusion.15 = f32[16,4,64,128]{3,2,1,0:T(8,128)S(1)} fusion(f32[16,4,128,64]{3,2,1,0:T(8,128)} %get-tuple-element.77, f32[4,16,128]{2,0,1:T(4,128)S(1)} %copy.110, f32[16,128,128]{2,1,0:T(8,128)S(1)} %convert_element_type.135, f32[4,128,64]{2,1,0:T(8,128)S(1)} %get-tuple-element.79, f32[16,4]{1,0:T(8,128)S(1)} %copy.107), kind=kOutput, calls=%fused_computation.22 | convolution fusion | flops 139460608 | bytes 5406976 | tf_op jit(solution)/shard_map/hctn,chnp->cthp/dot_general | solution.py:149
  405.5 2.7 add_bitcast_fusion
  409.4 2.4 fusion.23
  411.8 3.4 collective-permute-start.2
  415.2 2.2 collective-permute-done.2
  417.4 4.9 %collective-permute-start.3 = (f32[2048]{0:T(1024)S(1)}, f32[2048]{0:T(1024)S(1)}, u32[]{:S(2)}, u32[]{:S(2)}) collective-permute-start(f32[2048]{0:T(1024)S(1)} %add.124), channel_id=1, source_target_pairs={{0,2},{1,3},{2,0},{3,1},{4,6},{5,7},{6,4},{7,5},{8,10},{9,11},{10,... | collective-permute-start | bytes 24584 | tf_op jit(solution)/shard_map/ppermute | solution.py:44
  424.8 23.1 %all_to_all.19 = bf16[16,128,256]{1,2,0:T(8,128)(2,1)S(1)} all-to-all(bf16[16,128,256]{1,2,0:T(8,128)(2,1)S(1)} %copy_bitcast_fusion), channel_id=1, replica_groups=mesh['ctx'=32,'inner'=16] {'inner'}, dimensions={0} | all-to-all | bytes 2097152 | tf_op jit(solution)/shard_map/all_to_all | solution.py:162
  (241 shorter events, 85.7 us)
Async XLA Ops:
  6.5 34.9 %copy-start.5 = (bf16[64,4]{0,1:T(4,128)(2,1)S(1)}, bf16[64,4]{0,1:T(4,128)(2,1)}, u32[]{:S(2)}) copy-start(bf16[64,4]{0,1:T(4,128)(2,1)} %param.16) | copy-start | bytes 1540
  6.5 65.1 %copy-start.3 = (f32[5,2,512]{2,1,0:T(2,128)S(1)}, f32[5,2,512]{2,1,0:T(2,128)}, u32[]{:S(2)}) copy-start(f32[5,2,512]{2,1,0:T(2,128)} %param.18) | copy-start | bytes 61444
  6.5 72.4 %all-gather.8.cloned.1.call-start = ((), (), s32[]{:S(2)}) async-start(), calls=%async_computation.1 | async-start | bytes 2162688 | tf_op jit(solution)/shard_map/all_gather | solution.py:83
  7.3 140.0 %all-gather.10.cloned.1.call-start = ((), (), s32[]{:S(2)}) async-start(), calls=%async_computation.2 | async-start | bytes 4456448 | tf_op jit(solution)/shard_map/all_gather | solution.py:91
  38.8 34.0 %copy-start.7 = (f32[4]{0:T(128)S(1)}, f32[4]{0:T(128)}, u32[]{:S(2)}) copy-start(f32[4]{0:T(128)} %param.20) | copy-start | bytes 52
  38.8 34.0 %copy-start.4 = (f32[5,256]{1,0:T(8,128)S(1)}, f32[5,256]{1,0:T(8,128)}, u32[]{:S(2)}) copy-start(f32[5,256]{1,0:T(8,128)} %param.17) | copy-start | bytes 15364
  40.6 195.5 %all-gather.12.cloned.1.call-start = ((), (), s32[]{:S(2)}) async-start(), calls=%async_computation.3 | async-start | bytes 8912896 | tf_op jit(solution)/shard_map/all_gather | solution.py:104
  41.3 324.5 %all-gather.14.cloned.1.call-start = ((), (), s32[]{:S(2)}) async-start(), calls=%async_computation.4 | async-start | bytes 2162688 | tf_op jit(solution)/shard_map/all_gather | solution.py:24
  246.9 1.7 copy-start.1
  247.0 1.7 copy-start.6
  250.2 5.6 %collective-permute-start = (bf16[3,256]{0,1:T(8,128)(2,1)S(1)}, bf16[3,256]{0,1:T(8,128)(2,1)S(1)}, u32[]{:S(2)}, u32[]{:S(2)}) collective-permute-start(bf16[3,256]{0,1:T(8,128)(2,1)S(1)} %get-tuple-element.164), channel_id=1, source_target_pairs={{0,16},{16,32},{32,48},{48,64},{64,80},{80,96},{96,112},{112,128},... | collective-permute-start | bytes 4616 | tf_op jit(solution)/shard_map/ppermute | solution.py:18
  252.2 5.9 %collective-permute-start.1 = (bf16[3,2,128]{0,2,1:T(8,128)(2,1)S(1)}, bf16[3,2,128]{0,2,1:T(8,128)(2,1)S(1)}, u32[]{:S(2)}, u32[]{:S(2)}) collective-permute-start(bf16[3,2,128]{0,2,1:T(8,128)(2,1)S(1)} %bitcast.94), channel_id=1, source_target_pairs={{0,16},{16,32},{32,48},{48,64},{64,80},{80,96},{96,112},{112,128},... | collective-permute-start | bytes 4616 | tf_op jit(solution)/shard_map/ppermute | solution.py:18
  400.2 5.2 %copy-start = (f32[16,4,128,64]{3,2,1,0:T(8,128)S(1)}, f32[16,4,128,64]{3,2,1,0:T(8,128)}, u32[]{:S(2)}) copy-start(f32[16,4,128,64]{3,2,1,0:T(8,128)} %get-tuple-element.77) | copy-start | bytes 6291460
  400.2 5.2 %copy-start.2 = (f32[16,4,64,128]{3,2,1,0:T(8,128)S(1)}, f32[16,4,64,128]{3,2,1,0:T(8,128)}, u32[]{:S(2)}) copy-start(f32[16,4,64,128]{3,2,1,0:T(8,128)} %fusion.18) | copy-start | bytes 6291460
  411.8 5.5 %collective-permute-start.2 = (f32[2048]{0:T(1024)S(1)}, f32[2048]{0:T(1024)S(1)}, u32[]{:S(2)}, u32[]{:S(2)}) collective-permute-start(f32[2048]{0:T(1024)S(1)} %get-tuple-element.160), channel_id=1, source_target_pairs={{0,1},{1,0},{2,3},{3,2},{4,5},{5,4},{6,7},{7,6},{8,9},{9,8},{10,11... | collective-permute-start | bytes 24584 | tf_op jit(solution)/shard_map/ppermute | solution.py:44
  417.4 7.0 %collective-permute-start.3 = (f32[2048]{0:T(1024)S(1)}, f32[2048]{0:T(1024)S(1)}, u32[]{:S(2)}, u32[]{:S(2)}) collective-permute-start(f32[2048]{0:T(1024)S(1)} %add.124), channel_id=1, source_target_pairs={{0,2},{1,3},{2,0},{3,1},{4,6},{5,7},{6,4},{7,5},{8,10},{9,11},{10,... | collective-permute-start | bytes 24584 | tf_op jit(solution)/shard_map/ppermute | solution.py:44
Sparse Core Ops, SparseCore 0:
  9.5 69.3 all-gather.7
  81.9 65.2 all-gather.9
  150.3 85.8 all-gather.11
  294.5 71.2 all-gather.13
where the time goes:
time: 458 us; the launch traced here: 456 us
  waiting for transfers between devices  186 us (41%)
  blocking collectives  125 us (27%)
  local copies, waits for them, and re-layouts  48.5 us (11%)
  other arithmetic  41.3 us (9%)
  matrix products  26.4 us (6%)
  between operations  14.2 us (3%)
  starting transfers between devices  12.4 us (3%)
    all_gather x1, waiting for transfers between devices, on_device(): lax.all_gather(tokens, 'inner', axis=0, tiled=True)  85.3 us
    all_gather x1, waiting for transfers between devices, on_device(): full_cols = lax.all_gather(state_rows, 'inner', axis=2, tiled=True)  66.3 us
    unnamed x1, blocking collectives  42.4 us
    all_gather x1, blocking collectives, on_device(): lax.all_gather(state_weight, 'ctx', axis=0, tiled=True)  30.7 us
    dynamic_slice x60, local copies, waits for them, and re-layouts, one(): lax.dynamic_index_in_dim(a, turn, 0, False).astype(own.dtype)  29.4 us
    all_gather x1, blocking collectives, on_device(): lax.all_gather(step_weight, 'ctx', axis=0, tiled=True)  29.1 us
    all_to_all x1, blocking collectives, on_device(): lax.all_to_all(normed, 'inner', split_axis=0, concat_axis=1, tiled=True)  23.1 us
    all_gather x1, waiting for transfers between devices, entering(): lax.all_gather(a.astype(kind), axis)  22.2 us
  transfers between devices with their start and end apart: 8, of which 7 were waited for; matrix products, arithmetic and copies ran while one was open for 4% of the time, Pallas kernels for 0%

commit v1 on v0

--- a/solution.py
+++ b/solution.py
@@ -10,6 +10,24 @@
 CONV = 4
 SPAN = 128
 EPSILON = 1e-05
+
+
+def collect(shard, axis, dim):
+    ways, here, step = (lax.axis_size(axis), lax.axis_index(axis), shard.shape[dim])
+    shape = [n * ways if d == dim else n for d, n in enumerate(shard.shape)]
+    full = lax.dynamic_update_slice_in_dim(
+        jnp.zeros(shape, shard.dtype), shard, here * step, axis=dim
+    )
+    going_up = going_down = shard
+    for far in range(1, ways // 2 + 1):
+        going_up = lax.ppermute(going_up, axis, [(d, (d + 1) % ways) for d in range(ways)])
+        full = lax.dynamic_update_slice_in_dim(full, going_up, (here - far) % ways * step, axis=dim)
+        if 2 * far < ways:
+            going_down = lax.ppermute(going_down, axis, [(d, (d - 1) % ways) for d in range(ways)])
+            full = lax.dynamic_update_slice_in_dim(
+                full, going_down, (here + far) % ways * step, axis=dim
+            )
+    return full
 
 
 def passed_along(x, axis, by):
@@ -101,9 +119,7 @@
         axis=1,
     )
     projected = jnp.dot(
-        lax.all_gather(tokens, "inner", axis=0, tiled=True),
-        joined,
-        preferred_element_type=jnp.float32,
+        collect(tokens, "inner", 0), joined, preferred_element_type=jnp.float32
     ).astype(jnp.bfloat16)
     rows_total = projected.shape[0]
     gate_values = projected[:, :width_here]

time: 458 us -> 442 us (0.965)
  waiting for transfers between devices: 186 us -> 83.5 us
  starting transfers between devices: 12.4 us -> 77.9 us
  local copies, waits for them, and re-layouts: 48.5 us -> 69.4 us
    all_gather x1 -> x0, waiting for transfers between devices: 85.3 us -> none  [on_device(): lax.all_gather(tokens, 'inner', axis=0, tiled=True)]
    all_gather x1, waiting for transfers between devices: 66.3 us -> 0.01 us  [on_device(): full_cols = lax.all_gather(state_rows, 'inner', axis=2, tiled=True)]
    ppermute x0 -> x15, starting transfers between devices: none -> 65.6 us  [the longest x7 48.8 us: collect(): lax.ppermute(going_down, axis, [(d, (d - 1) % ways) for d in range(ways)])]
    ppermute x0 -> x15, waiting for transfers between devices: none -> 58.6 us  [the longest x7 30.4 us: collect(): lax.ppermute(going_down, axis, [(d, (d - 1) % ways) for d in range(ways)])]
    dynamic_update_slice x0 -> x16, local copies, waits for them, and re-layouts: none -> 16.7 us  [the longest x8 8.89 us: collect(): lax.dynamic_update_slice_in_dim(full, going_up, (here - far) % ways * ste...]
    all_gather x1, waiting for transfers between devices: 6.12 us -> 0.01 us  [on_device(): lax.all_gather(project_weight, 'ctx', axis=0, tiled=True)]
  transfers between devices with their start and end apart: 8 -> 22, of which waited for: 7 -> 12; matrix products, arithmetic and copies ran while one was open for 4% -> 8% of each run, Pallas kernels for 0% -> 0%
where the time goes in v1:
time: 442 us; the launch traced here: 439 us
  blocking collectives  126 us (29%)
  waiting for transfers between devices  83.5 us (19%)
  starting transfers between devices  77.9 us (18%)
  local copies, waits for them, and re-layouts  69.4 us (16%)
  other arithmetic  41.3 us (9%)
  matrix products  25.3 us (6%)
  between operations  14.6 us (3%)
    ppermute x7, starting transfers between devices, collect(): lax.ppermute(going_down, axis, [(d, (d - 1) % ways) for d in range(ways)])  48.8 us
    unnamed x1, blocking collectives  42.7 us
    all_gather x1, blocking collectives, on_device(): lax.all_gather(state_weight, 'ctx', axis=0, tiled=True)  30.7 us
    ppermute x7, waiting for transfers between devices, collect(): lax.ppermute(going_down, axis, [(d, (d - 1) % ways) for d in range(ways)])  30.4 us
    dynamic_slice x60, local copies, waits for them, and re-layouts, one(): lax.dynamic_index_in_dim(a, turn, 0, False).astype(own.dtype)  29.4 us
    all_gather x1, blocking collectives, on_device(): lax.all_gather(step_weight, 'ctx', axis=0, tiled=True)  29.1 us
    ppermute x8, waiting for transfers between devices, collect(): lax.ppermute(going_up, axis, [(d, (d + 1) % ways) for d in range(ways)])  28.1 us
    all_to_all x1, blocking collectives, on_device(): lax.all_to_all(normed, 'inner', split_axis=0, concat_axis=1, tiled=True)  23.1 us
  transfers between devices with their start and end apart: 22, of which 12 were waited for; matrix products, arithmetic and copies ran while one was open for 8% of the time, Pallas kernels for 0%

profile of v1, /device:TPU:480, one launch (start us, length us, event | category | flops | bytes accessed | tf_op | source)
XLA Modules:
  0.0 439.1 jit_solution(16131535753167016374)
XLA Ops:
  8.1 30.7 %all_gather.23 = bf16[2048,2,32]{2,1,0:T(2,128)(2,1)S(1)} all-gather(bf16[64,2,32]{2,1,0:T(2,128)(2,1)S(1)} %copy.91), channel_id=1, replica_groups=mesh['ctx'=32,'inner'=16] {'ctx'}, dimensions={0}, use_global_device_ids=true | all-gather | bytes 270336 | tf_op jit(solution)/shard_map/all_gather | solution.py:102
  44.0 5.8 %collective-permute-start.1 = (bf16[128,2048]{1,0:T(8,128)(2,1)S(1)}, bf16[128,2048]{1,0:T(8,128)(2,1)S(1)}, u32[]{:S(2)}, u32[]{:S(2)}) collective-permute-start(bf16[128,2048]{1,0:T(8,128)(2,1)S(1)} %copy-done.3), channel_id=1, source_target_pairs={{0,15},{1,0},{2,1},{3,2},{4,3},{5,4},{6,5},{7,6},{8,7},{9,8},{10,9... | collective-permute-start | bytes 1572872 | tf_op jit(solution)/shard_map/ppermute | solution.py:26
  49.8 10.2 %collective-permute-done = bf16[128,2048]{1,0:T(8,128)(2,1)S(1)} collective-permute-done((bf16[128,2048]{1,0:T(8,128)(2,1)S(1)}, bf16[128,2048]{1,0:T(8,128)(2,1)S(1)}, u32[]{:S(2)}, u32[]{:S(2)}) %collective-permute-start) | collective-permute-done | bytes 524320 | tf_op jit(solution)/shard_map/ppermute | solution.py:23
  62.0 7.2 %collective-permute-start.3 = (bf16[128,2048]{1,0:T(8,128)(2,1)S(1)}, bf16[128,2048]{1,0:T(8,128)(2,1)S(1)}, u32[]{:S(2)}, u32[]{:S(2)}) collective-permute-start(bf16[128,2048]{1,0:T(8,128)(2,1)S(1)} %collective-permute-done.1), channel_id=1, source_target_pairs={{0,15},{1,0},{2,1},{3,2},{4,3},{5,4},{6,5},{7,6},{8,7},{9,8},{10,9... | collective-permute-start | bytes 1572872 | tf_op jit(solution)/shard_map/ppermute | solution.py:26
  69.2 9.4 %collective-permute-done.2 = bf16[128,2048]{1,0:T(8,128)(2,1)S(1)} collective-permute-done((bf16[128,2048]{1,0:T(8,128)(2,1)S(1)}, bf16[128,2048]{1,0:T(8,128)(2,1)S(1)}, u32[]{:S(2)}, u32[]{:S(2)}) %collective-permute-start.2) | collective-permute-done | bytes 524320 | tf_op jit(solution)/shard_map/ppermute | solution.py:23
  85.7 7.4 %collective-permute-start.5 = (bf16[128,2048]{1,0:T(8,128)(2,1)S(1)}, bf16[128,2048]{1,0:T(8,128)(2,1)}, u32[]{:S(2)}, u32[]{:S(2)}) collective-permute-start(bf16[128,2048]{1,0:T(8,128)(2,1)S(1)} %collective-permute-done.3), channel_id=1, source_target_pairs={{0,15},{1,0},{2,1},{3,2},{4,3},{5,4},{6,5},{7,6},{8,7},{9,8},{10,9... | collective-permute-start | bytes 1572872 | tf_op jit(solution)/shard_map/ppermute | solution.py:26
  98.5 29.1 %all-gather.2 = bf16[32,64,4]{1,2,0:T(4,128)(2,1)S(1)} all-gather(bf16[1,64,4]{1,2,0:T(4,128)(2,1)S(1)} %bitcast.100), channel_id=1, replica_groups=mesh['ctx'=32,'inner'=16] {'ctx'}, dimensions={0}, use_global_device_ids=true | all-gather | bytes 16896 | tf_op jit(solution)/shard_map/all_gather | solution.py:103
  131.9 7.2 %collective-permute-start.7 = (bf16[128,2048]{1,0:T(8,128)(2,1)}, bf16[128,2048]{1,0:T(8,128)(2,1)S(1)}, u32[]{:S(2)}, u32[]{:S(2)}) collective-permute-start(bf16[128,2048]{1,0:T(8,128)(2,1)} %collective-permute-done.5), channel_id=1, source_target_pairs={{0,15},{1,0},{2,1},{3,2},{4,3},{5,4},{6,5},{7,6},{8,7},{9,8},{10,9... | collective-permute-start | bytes 1572872 | tf_op jit(solution)/shard_map/ppermute | solution.py:26
  143.6 15.0 %collective-permute-done.7 = bf16[128,2048]{1,0:T(8,128)(2,1)S(1)} collective-permute-done((bf16[128,2048]{1,0:T(8,128)(2,1)}, bf16[128,2048]{1,0:T(8,128)(2,1)S(1)}, u32[]{:S(2)}, u32[]{:S(2)}) %collective-permute-start.7) | collective-permute-done | bytes 524320 | tf_op jit(solution)/shard_map/ppermute | solution.py:26
  158.6 5.8 %collective-permute-start.9 = (bf16[128,2048]{1,0:T(8,128)(2,1)S(1)}, bf16[128,2048]{1,0:T(8,128)(2,1)S(1)}, u32[]{:S(2)}, u32[]{:S(2)}) collective-permute-start(bf16[128,2048]{1,0:T(8,128)(2,1)S(1)} %collective-permute-done.7), channel_id=1, source_target_pairs={{0,15},{1,0},{2,1},{3,2},{4,3},{5,4},{6,5},{7,6},{8,7},{9,8},{10,9... | collective-permute-start | bytes 1572872 | tf_op jit(solution)/shard_map/ppermute | solution.py:26
  170.9 4.6 %collective-permute-done.9 = bf16[128,2048]{1,0:T(8,128)(2,1)S(1)} collective-permute-done((bf16[128,2048]{1,0:T(8,128)(2,1)S(1)}, bf16[128,2048]{1,0:T(8,128)(2,1)S(1)}, u32[]{:S(2)}, u32[]{:S(2)}) %collective-permute-start.9) | collective-permute-done | bytes 524320 | tf_op jit(solution)/shard_map/ppermute | solution.py:26
  175.5 7.7 %collective-permute-start.11 = (bf16[128,2048]{1,0:T(8,128)(2,1)S(1)}, bf16[128,2048]{1,0:T(8,128)(2,1)S(1)}, u32[]{:S(2)}, u32[]{:S(2)}) collective-permute-start(bf16[128,2048]{1,0:T(8,128)(2,1)S(1)} %collective-permute-done.9), channel_id=1, source_target_pairs={{0,15},{1,0},{2,1},{3,2},{4,3},{5,4},{6,5},{7,6},{8,7},{9,8},{10,9... | collective-permute-start | bytes 1572872 | tf_op jit(solution)/shard_map/ppermute | solution.py:26
  187.7 5.9 %collective-permute-done.11 = bf16[128,2048]{1,0:T(8,128)(2,1)S(1)} collective-permute-done((bf16[128,2048]{1,0:T(8,128)(2,1)S(1)}, bf16[128,2048]{1,0:T(8,128)(2,1)S(1)}, u32[]{:S(2)}, u32[]{:S(2)}) %collective-permute-start.11) | collective-permute-done | bytes 524320 | tf_op jit(solution)/shard_map/ppermute | solution.py:26
  193.6 7.7 %collective-permute-start.13 = (bf16[128,2048]{1,0:T(8,128)(2,1)S(1)}, bf16[128,2048]{1,0:T(8,128)(2,1)S(1)}, u32[]{:S(2)}, u32[]{:S(2)}) collective-permute-start(bf16[128,2048]{1,0:T(8,128)(2,1)S(1)} %collective-permute-done.11), channel_id=1, source_target_pairs={{0,15},{1,0},{2,1},{3,2},{4,3},{5,4},{6,5},{7,6},{8,7},{9,8},{10,9... | collective-permute-start | bytes 1572872 | tf_op jit(solution)/shard_map/ppermute | solution.py:26
  205.7 4.9 %collective-permute-done.13 = bf16[128,2048]{1,0:T(8,128)(2,1)S(1)} collective-permute-done((bf16[128,2048]{1,0:T(8,128)(2,1)S(1)}, bf16[128,2048]{1,0:T(8,128)(2,1)S(1)}, u32[]{:S(2)}, u32[]{:S(2)}) %collective-permute-start.13) | collective-permute-done | bytes 524320 | tf_op jit(solution)/shard_map/ppermute | solution.py:26
  213.5 5.4 %collective-permute-done.14 = bf16[128,2048]{1,0:T(8,128)(2,1)S(1)} collective-permute-done((bf16[128,2048]{1,0:T(8,128)(2,1)S(1)}, bf16[128,2048]{1,0:T(8,128)(2,1)S(1)}, u32[]{:S(2)}, u32[]{:S(2)}) %collective-permute-start.14) | collective-permute-done | bytes 524320 | tf_op jit(solution)/shard_map/ppermute | solution.py:23
  223.4 9.7 %fusion.9 = bf16[2048,772]{0,1:T(8,128)(2,1)S(1)} fusion(bf16[2048,2048]{1,0:T(8,128)(2,1)} %constant_dynamic-update-slice_fusion, bf16[2048,4]{1,0:T(8,128)(2,1)} %bitcast.90, bf16[2048,256]{1,0:T(8,128)(2,1)} %copy.95, bf16[2048,512]{1,0:T(8,128)(2,1)S(1)} %bitcast.89), kind=kOutput, calls=%fused_computation.20 | convolution fusion | flops 6487072768 | bytes 14712832 | tf_op jit(solution)/shard_map/dot_general | solution.py:121
  250.9 28.8 %while.26 = (s32[]{:T(128)}, f32[4,128,64]{2,1,0:T(8,128)S(1)}, f32[16,4,128,64]{3,2,1,0:T(8,128)}, f32[16,4]{1,0:T(8,128)S(1)}, f32[16,4,128,64]{3,2,1,0:T(8,128)}, /*index=5*/s32[]{:T(128)}, s32[]{:T(128)}) while((s32[]{:T(128)}, f32[4,128,64]{2,1,0:T(8,128)S(1)}, f32[16,4,128,64]{3,2,1,0:T(8,128)}, f32[16,4]{1,0:T(8,128)S(1)}, ...), condition=%wide.region_2.3_spmd.clone, body=%wide.region_1.2_spmd.clone.sunk | while | flops 131075 | bytes 787088 | solution.py:152
  282.9 42.7 %all-reduce = bf16[128]{0:T(256)(128)(2,1)S(1)} all-reduce(bf16[128]{0:T(256)(128)(2,1)S(1)} %dynamic-update-slice), channel_id=2, replica_groups=mesh['ctx'=32,'inner'=16] {'ctx'}, use_global_device_ids=true, to_apply=%add | all-reduce | flops 128 | bytes 512
  329.9 19.3 %all-gather.11.cloned.1.call-done = bf16[128,128,64]{1,2,0:T(8,128)(2,1)} async-done(((bf16[4,128,64]{1,2,0:T(8,128)(2,1)}), bf16[128,128,64]{1,2,0:T(8,128)(2,1)}) %all-gather.11.cloned.1.call-update) | async-done | bytes 2097168 | tf_op jit(solution)/shard_map/all_gather | solution.py:42
  349.2 34.4 %while.25 = (s32[]{:T(128)}, f32[4,128,64]{2,1,0:T(8,128)S(1)}, s32[]{:T(128)}, bf16[32,4]{1,0:T(8,128)(2,1)S(1)}, bf16[32,4,128,64]{2,3,1,0:T(8,128)(2,1)}, /*index=5*/s32[]{:T(128)}, s32[]{:T(128)}, s32[]{:T(128)}) while((s32[]{:T(128)}, f32[4,128,64]{2,1,0:T(8,128)S(1)}, s32[]{:T(128)}, bf16[32,4]{1,0:T(8,128)(2,1)S(1)}, ...), condition=%wide.region_6.7_spmd, body=%wide.region_5.6_spmd.sunk | while | flops 98313 | bytes 589991 | solution.py:56
  383.6 5.2 %fusion.12 = f32[16,4,64,128]{3,2,1,0:T(8,128)S(1)} fusion(f32[16,4,128,64]{3,2,1,0:T(8,128)} %get-tuple-element.77, f32[4,16,128]{2,0,1:T(4,128)S(1)} %copy.110, f32[16,128,128]{2,1,0:T(8,128)S(1)} %convert_element_type.131, f32[4,128,64]{2,1,0:T(8,128)S(1)} %get-tuple-element.79, f32[16,4]{1,0:T(8,128)S(1)} %copy.107), kind=kOutput, calls=%fused_computation.21 | convolution fusion | flops 139460608 | bytes 5406976 | tf_op jit(solution)/shard_map/hctn,chnp->cthp/dot_general | solution.py:165
  400.7 4.9 %collective-permute-start.18 = (f32[2048]{0:T(1024)S(1)}, f32[2048]{0:T(1024)S(1)}, u32[]{:S(2)}, u32[]{:S(2)}) collective-permute-start(f32[2048]{0:T(1024)S(1)} %add.285), channel_id=1, source_target_pairs={{0,2},{1,3},{2,0},{3,1},{4,6},{5,7},{6,4},{7,5},{8,10},{9,11},{10,... | collective-permute-start | bytes 24584 | tf_op jit(solution)/shard_map/ppermute | solution.py:62
  408.2 23.1 %all_to_all.19 = bf16[16,128,256]{1,2,0:T(8,128)(2,1)S(1)} all-to-all(bf16[16,128,256]{1,2,0:T(8,128)(2,1)S(1)} %copy_bitcast_fusion), channel_id=1, replica_groups=mesh['ctx'=32,'inner'=16] {'inner'}, dimensions={0} | all-to-all | bytes 2097152 | tf_op jit(solution)/shard_map/all_to_all | solution.py:178
  (293 shorter events, 154.1 us)
Async XLA Ops:
  6.5 204.9 %all-gather.7.cloned.1.call-start = ((), (), s32[]{:S(2)}) async-start(), calls=%async_computation.1 | async-start | bytes 2162688 | tf_op jit(solution)/shard_map/all_gather | solution.py:101
  7.3 212.5 %all-gather.9.cloned.1.call-start = ((), (), s32[]{:S(2)}) async-start(), calls=%async_computation.2 | async-start | bytes 4456448 | tf_op jit(solution)/shard_map/all_gather | solution.py:109
  40.6 308.6 %all-gather.11.cloned.1.call-start = ((), (), s32[]{:S(2)}) async-start(), calls=%async_computation.3 | async-start | bytes 2162688 | tf_op jit(solution)/shard_map/all_gather | solution.py:42
  40.7 19.4 %collective-permute-start = (bf16[128,2048]{1,0:T(8,128)(2,1)S(1)}, bf16[128,2048]{1,0:T(8,128)(2,1)S(1)}, u32[]{:S(2)}, u32[]{:S(2)}) collective-permute-start(bf16[128,2048]{1,0:T(8,128)(2,1)S(1)} %copy-done.3), channel_id=1, source_target_pairs={{0,1},{1,2},{2,3},{3,4},{4,5},{5,6},{6,7},{7,8},{8,9},{9,10},{10,1... | collective-permute-start | bytes 1572872 | tf_op jit(solution)/shard_map/ppermute | solution.py:23
  44.0 18.0 %collective-permute-start.1 = (bf16[128,2048]{1,0:T(8,128)(2,1)S(1)}, bf16[128,2048]{1,0:T(8,128)(2,1)S(1)}, u32[]{:S(2)}, u32[]{:S(2)}) collective-permute-start(bf16[128,2048]{1,0:T(8,128)(2,1)S(1)} %copy-done.3), channel_id=1, source_target_pairs={{0,15},{1,0},{2,1},{3,2},{4,3},{5,4},{6,5},{7,6},{8,7},{9,8},{10,9... | collective-permute-start | bytes 1572872 | tf_op jit(solution)/shard_map/ppermute | solution.py:26
  60.0 18.6 %collective-permute-start.2 = (bf16[128,2048]{1,0:T(8,128)(2,1)S(1)}, bf16[128,2048]{1,0:T(8,128)(2,1)S(1)}, u32[]{:S(2)}, u32[]{:S(2)}) collective-permute-start(bf16[128,2048]{1,0:T(8,128)(2,1)S(1)} %collective-permute-done), channel_id=1, source_target_pairs={{0,1},{1,2},{2,3},{3,4},{4,5},{5,6},{6,7},{7,8},{8,9},{9,10},{10,1... | collective-permute-start | bytes 1572872 | tf_op jit(solution)/shard_map/ppermute | solution.py:23
  62.0 23.8 %collective-permute-start.3 = (bf16[128,2048]{1,0:T(8,128)(2,1)S(1)}, bf16[128,2048]{1,0:T(8,128)(2,1)S(1)}, u32[]{:S(2)}, u32[]{:S(2)}) collective-permute-start(bf16[128,2048]{1,0:T(8,128)(2,1)S(1)} %collective-permute-done.1), channel_id=1, source_target_pairs={{0,15},{1,0},{2,1},{3,2},{4,3},{5,4},{6,5},{7,6},{8,7},{9,8},{10,9... | collective-permute-start | bytes 1572872 | tf_op jit(solution)/shard_map/ppermute | solution.py:26
  78.6 17.7 %collective-permute-start.4 = (bf16[128,2048]{1,0:T(8,128)(2,1)S(1)}, bf16[128,2048]{1,0:T(8,128)(2,1)S(1)}, u32[]{:S(2)}, u32[]{:S(2)}) collective-permute-start(bf16[128,2048]{1,0:T(8,128)(2,1)S(1)} %collective-permute-done.2), channel_id=1, source_target_pairs={{0,1},{1,2},{2,3},{3,4},{4,5},{5,6},{6,7},{7,8},{8,9},{9,10},{10,1... | collective-permute-start | bytes 1572872 | tf_op jit(solution)/shard_map/ppermute | solution.py:23
  84.9 43.8 %copy-start.7 = (f32[5,2,512]{2,1,0:T(2,128)S(1)}, f32[5,2,512]{2,1,0:T(2,128)}, u32[]{:S(2)}) copy-start(f32[5,2,512]{2,1,0:T(2,128)} %param.18) | copy-start | bytes 61444
  85.7 53.4 %copy-start.5 = (bf16[128,2048]{1,0:T(8,128)(2,1)S(1)}, bf16[128,2048]{1,0:T(8,128)(2,1)}, u32[]{:S(2)}) copy-start(bf16[128,2048]{1,0:T(8,128)(2,1)} %copy-done.4) | copy-start | bytes 1572868
  85.7 46.1 %collective-permute-start.5 = (bf16[128,2048]{1,0:T(8,128)(2,1)S(1)}, bf16[128,2048]{1,0:T(8,128)(2,1)}, u32[]{:S(2)}, u32[]{:S(2)}) collective-permute-start(bf16[128,2048]{1,0:T(8,128)(2,1)S(1)} %collective-permute-done.3), channel_id=1, source_target_pairs={{0,15},{1,0},{2,1},{3,2},{4,3},{5,4},{6,5},{7,6},{8,7},{9,8},{10,9... | collective-permute-start | bytes 1572872 | tf_op jit(solution)/shard_map/ppermute | solution.py:26
  96.3 43.7 %collective-permute-start.6 = (bf16[128,2048]{1,0:T(8,128)(2,1)S(1)}, bf16[128,2048]{1,0:T(8,128)(2,1)}, u32[]{:S(2)}, u32[]{:S(2)}) collective-permute-start(bf16[128,2048]{1,0:T(8,128)(2,1)S(1)} %collective-permute-done.4), channel_id=1, source_target_pairs={{0,1},{1,2},{2,3},{3,4},{4,5},{5,6},{6,7},{7,8},{8,9},{9,10},{10,1... | collective-permute-start | bytes 1572872 | tf_op jit(solution)/shard_map/ppermute | solution.py:23
  131.9 26.7 %collective-permute-start.7 = (bf16[128,2048]{1,0:T(8,128)(2,1)}, bf16[128,2048]{1,0:T(8,128)(2,1)S(1)}, u32[]{:S(2)}, u32[]{:S(2)}) collective-permute-start(bf16[128,2048]{1,0:T(8,128)(2,1)} %collective-permute-done.5), channel_id=1, source_target_pairs={{0,15},{1,0},{2,1},{3,2},{4,3},{5,4},{6,5},{7,6},{8,7},{9,8},{10,9... | collective-permute-start | bytes 1572872 | tf_op jit(solution)/shard_map/ppermute | solution.py:26
  139.9 25.3 %collective-permute-start.8 = (bf16[128,2048]{1,0:T(8,128)(2,1)}, bf16[128,2048]{1,0:T(8,128)(2,1)S(1)}, u32[]{:S(2)}, u32[]{:S(2)}) collective-permute-start(bf16[128,2048]{1,0:T(8,128)(2,1)} %collective-permute-done.6), channel_id=1, source_target_pairs={{0,1},{1,2},{2,3},{3,4},{4,5},{5,6},{6,7},{7,8},{8,9},{9,10},{10,1... | collective-permute-start | bytes 1572872 | tf_op jit(solution)/shard_map/ppermute | solution.py:23
  158.6 17.0 %collective-permute-start.9 = (bf16[128,2048]{1,0:T(8,128)(2,1)S(1)}, bf16[128,2048]{1,0:T(8,128)(2,1)S(1)}, u32[]{:S(2)}, u32[]{:S(2)}) collective-permute-start(bf16[128,2048]{1,0:T(8,128)(2,1)S(1)} %collective-permute-done.7), channel_id=1, source_target_pairs={{0,15},{1,0},{2,1},{3,2},{4,3},{5,4},{6,5},{7,6},{8,7},{9,8},{10,9... | collective-permute-start | bytes 1572872 | tf_op jit(solution)/shard_map/ppermute | solution.py:26
  165.2 18.9 %collective-permute-start.10 = (bf16[128,2048]{1,0:T(8,128)(2,1)S(1)}, bf16[128,2048]{1,0:T(8,128)(2,1)S(1)}, u32[]{:S(2)}, u32[]{:S(2)}) collective-permute-start(bf16[128,2048]{1,0:T(8,128)(2,1)S(1)} %collective-permute-done.8), channel_id=1, source_target_pairs={{0,1},{1,2},{2,3},{3,4},{4,5},{5,6},{6,7},{7,8},{8,9},{9,10},{10,1... | collective-permute-start | bytes 1572872 | tf_op jit(solution)/shard_map/ppermute | solution.py:23
  175.5 18.0 %collective-permute-start.11 = (bf16[128,2048]{1,0:T(8,128)(2,1)S(1)}, bf16[128,2048]{1,0:T(8,128)(2,1)S(1)}, u32[]{:S(2)}, u32[]{:S(2)}) collective-permute-start(bf16[128,2048]{1,0:T(8,128)(2,1)S(1)} %collective-permute-done.9), channel_id=1, source_target_pairs={{0,15},{1,0},{2,1},{3,2},{4,3},{5,4},{6,5},{7,6},{8,7},{9,8},{10,9... | collective-permute-start | bytes 1572872 | tf_op jit(solution)/shard_map/ppermute | solution.py:26
  184.1 18.0 %collective-permute-start.12 = (bf16[128,2048]{1,0:T(8,128)(2,1)S(1)}, bf16[128,2048]{1,0:T(8,128)(2,1)S(1)}, u32[]{:S(2)}, u32[]{:S(2)}) collective-permute-start(bf16[128,2048]{1,0:T(8,128)(2,1)S(1)} %collective-permute-done.10), channel_id=1, source_target_pairs={{0,1},{1,2},{2,3},{3,4},{4,5},{5,6},{6,7},{7,8},{8,9},{9,10},{10,1... | collective-permute-start | bytes 1572872 | tf_op jit(solution)/shard_map/ppermute | solution.py:23
  193.6 17.1 %collective-permute-start.13 = (bf16[128,2048]{1,0:T(8,128)(2,1)S(1)}, bf16[128,2048]{1,0:T(8,128)(2,1)S(1)}, u32[]{:S(2)}, u32[]{:S(2)}) collective-permute-start(bf16[128,2048]{1,0:T(8,128)(2,1)S(1)} %collective-permute-done.11), channel_id=1, source_target_pairs={{0,15},{1,0},{2,1},{3,2},{4,3},{5,4},{6,5},{7,6},{8,7},{9,8},{10,9... | collective-permute-start | bytes 1572872 | tf_op jit(solution)/shard_map/ppermute | solution.py:26
  202.1 16.8 %collective-permute-start.14 = (bf16[128,2048]{1,0:T(8,128)(2,1)S(1)}, bf16[128,2048]{1,0:T(8,128)(2,1)S(1)}, u32[]{:S(2)}, u32[]{:S(2)}) collective-permute-start(bf16[128,2048]{1,0:T(8,128)(2,1)S(1)} %collective-permute-done.12), channel_id=1, source_target_pairs={{0,1},{1,2},{2,3},{3,4},{4,5},{5,6},{6,7},{7,8},{8,9},{9,10},{10,1... | collective-permute-start | bytes 1572872 | tf_op jit(solution)/shard_map/ppermute | solution.py:23
  236.3 5.6 %collective-permute-start.15 = (bf16[3,256]{0,1:T(8,128)(2,1)S(1)}, bf16[3,256]{0,1:T(8,128)(2,1)S(1)}, u32[]{:S(2)}, u32[]{:S(2)}) collective-permute-start(bf16[3,256]{0,1:T(8,128)(2,1)S(1)} %get-tuple-element.164), channel_id=1, source_target_pairs={{0,16},{16,32},{32,48},{48,64},{64,80},{80,96},{96,112},{112,128},... | collective-permute-start | bytes 4616 | tf_op jit(solution)/shard_map/ppermute | solution.py:36
  238.3 5.9 %collective-permute-start.16 = (bf16[3,2,128]{0,2,1:T(8,128)(2,1)S(1)}, bf16[3,2,128]{0,2,1:T(8,128)(2,1)S(1)}, u32[]{:S(2)}, u32[]{:S(2)}) collective-permute-start(bf16[3,2,128]{0,2,1:T(8,128)(2,1)S(1)} %bitcast.92), channel_id=1, source_target_pairs={{0,16},{16,32},{32,48},{48,64},{64,80},{80,96},{96,112},{112,128},... | collective-permute-start | bytes 4616 | tf_op jit(solution)/shard_map/ppermute | solution.py:36
  395.2 5.5 %collective-permute-start.17 = (f32[2048]{0:T(1024)S(1)}, f32[2048]{0:T(1024)S(1)}, u32[]{:S(2)}, u32[]{:S(2)}) collective-permute-start(f32[2048]{0:T(1024)S(1)} %get-tuple-element.160), channel_id=1, source_target_pairs={{0,1},{1,0},{2,3},{3,2},{4,5},{5,4},{6,7},{7,6},{8,9},{9,8},{10,11... | collective-permute-start | bytes 24584 | tf_op jit(solution)/shard_map/ppermute | solution.py:62
  400.7 7.0 %collective-permute-start.18 = (f32[2048]{0:T(1024)S(1)}, f32[2048]{0:T(1024)S(1)}, u32[]{:S(2)}, u32[]{:S(2)}) collective-permute-start(f32[2048]{0:T(1024)S(1)} %add.285), channel_id=1, source_target_pairs={{0,2},{1,3},{2,0},{3,1},{4,6},{5,7},{6,4},{7,5},{8,10},{9,11},{10,... | collective-permute-start | bytes 24584 | tf_op jit(solution)/shard_map/ppermute | solution.py:62
  (10 other events, 143.9 us)
Sparse Core Ops, SparseCore 0:
  9.5 69.4 all-gather.6
  82.0 81.0 all-gather.8
  280.6 68.4 all-gather.10
